TPU v7x, 128 devices: a whole 4x4x4 slice. The times are simulated.
128 devices in a mesh: dp: 16 (over y_lo, x, core), fsdp: 8 (over y_hi, z).
Axes of the slice: x: 4, y: 4 (y_hi: 2, y_lo: 2; y = y_hi * 2 + y_lo), z: 4, core: 2. Of those that a mesh axis runs over, the one named last changes fastest.
Arguments:
- tokens: bfloat16 [32768, 1024], P(('dp', 'fsdp')), may hold values from -24 to 24
- positions: int32 [32768], P(('dp', 'fsdp')), may hold values from 0 to 255, as said below
- w_query: bfloat16 [1024, 2048], P('dp', 'fsdp'), may hold values from -0.1875 to 0.1875
- w_key: bfloat16 [1024, 1024], P('dp', 'fsdp'), may hold values from -0.1875 to 0.1875
- w_value: bfloat16 [1024, 1024], P('dp', 'fsdp'), may hold values from -0.1875 to 0.1875
- w_out: bfloat16 [2048, 1024], P('fsdp', 'dp'), may hold values from -0.125 to 0.125
- w_gate: bfloat16 [1024, 3072], P('dp', 'fsdp'), may hold values from -0.1875 to 0.1875
- w_up: bfloat16 [1024, 3072], P('dp', 'fsdp'), may hold values from -0.1875 to 0.1875
- w_down: bfloat16 [3072, 1024], P('fsdp', 'dp'), may hold values from -0.109375 to 0.109375
- query_gain: bfloat16 [128], P('dp'), may hold values from 1 to 2
- key_gain: bfloat16 [128], P('dp'), may hold values from 1 to 2
- attn_gain: bfloat16 [1024], P('dp'), may hold values from 0.5 to 2
- ffn_gain: bfloat16 [1024], P('dp'), may hold values from 0.5 to 2
- cotangent: bfloat16 [32768, 1024], P(('dp', 'fsdp')), may hold values from -24 to 24
Outputs:
- mixed: bfloat16 [32768, 1024], P(('dp', 'fsdp'))
- tokens_grad: float32 [32768, 1024], P(('dp', 'fsdp'))
- w_query_grad: float32 [1024, 2048], P('dp', 'fsdp')
- w_key_grad: float32 [1024, 1024], P('dp', 'fsdp')
- w_value_grad: float32 [1024, 1024], P('dp', 'fsdp')
- w_out_grad: float32 [2048, 1024], P('fsdp', 'dp')
- w_gate_grad: float32 [1024, 3072], P('dp', 'fsdp')
- w_up_grad: float32 [1024, 3072], P('dp', 'fsdp')
- w_down_grad: float32 [3072, 1024], P('fsdp', 'dp')
- query_gain_grad: float32 [128], P('dp')
- key_gain_grad: float32 [128], P('dp')
- attn_gain_grad: float32 [1024], P('dp')
- ffn_gain_grad: float32 [1024], P('dp')
Inputs may be any that keep to these rules, and one draw needn't show every extreme that they name: Every aligned block of 256 tokens holds whole sequences: each sequence's positions run 0, 1, 2, ... in consecutive slots, and every block begins with 0. In every draw one block holds a single sequence of 256 tokens.
All inputs are finite; a program needn't handle non-finite values.
Results may differ from a plain program's by a relative error of at most 0.025.
Values may be sent and summed in bfloat16 or wider, within the bound.
A program may use at most 192 MiB of HBM per device.

v0:
```python
import math

import numpy as np
import jax
import jax.numpy as jnp
from jax import lax
from jax.experimental import pallas as pl
from jax.experimental.pallas import tpu as pltpu
from jax.sharding import PartitionSpec as P

MESH = pl.DeviceIdType.MESH
F32, BF = jnp.float32, jnp.bfloat16
D, HD, TOK = 1024, 128, 256
EPS = 1e-6
ROPE_BASE = 1000000.0
GATHER = ("q0", "q1", "k", "v", "o0", "o1", "g0", "u0", "g1", "u1", "g2", "u2", "d0", "d1", "d2")
REDUCE = ("d0", "d1", "d2", "g0", "u0", "g1", "u1", "g2", "u2", "o0", "o1", "q0", "q1", "k", "v")
ORDERS = ("xyz", "yzx", "zxy")
SHARD = ("q0", "q1", "k", "v", "o0", "o1", "g0", "g1", "g2", "u0", "u1", "u2", "d0", "d1", "d2")
UNIT = {name: i for i, name in enumerate(SHARD)}
NU = len(SHARD)
LATENCY, REDUCE_LATENCY = 2.6, 10.0
GATHER_BACKLOG, REDUCE_BACKLOG, AHEAD = 1000.0, 6.0, 2
SPARE = 4
PLACE = dict(
    d0=15, d1=16, d2="d0", g0="d1", u0="d2", g1="g0", u1="u0", g2="g1", u2="u1", o0="g2", o1="u2", q0="o0", q1="o1",
    k=17, v=18,
)


def nn(a, b):
    return jnp.dot(a, b, preferred_element_type=F32)


def nt(a, b):
    return lax.dot_general(a, b, (((1,), (1,)), ((), ())), preferred_element_type=F32)


def tn(a, b):
    return lax.dot_general(a, b, (((0,), (0,)), ((), ())), preferred_element_type=F32)


def when(cond, body):
    if cond is None:
        body()
    else:
        pl.when(cond)(body)


class Place:
    def __init__(self):
        dp, fs = lax.axis_index("dp"), lax.axis_index("fsdp")
        self.c = lax.rem(dp, 2)
        self.x = lax.rem(lax.div(dp, 2), 4)
        self.yl = lax.div(dp, 8)
        self.yh = lax.div(fs, 4)
        self.z = lax.rem(fs, 4)
        self.y = self.yh * 2 + self.yl
        self.zi = lax.div(self.z, 2)
        self.own = lax.rem(self.z, 2) == self.c
        self.other = lax.rem(self.z, 2) != self.c

    def device(self, x, y, z, c):
        return (lax.rem(y, 2) * 8 + x * 2 + c, lax.div(y, 2) * 4 + z)

    def step(self, axis, by):
        go = lambda v: lax.rem(v + (by + 4), 4)
        return self.device(
            go(self.x) if axis == "x" else self.x,
            go(self.y) if axis == "y" else self.y,
            go(self.z) if axis == "z" else self.z,
            self.c,
        )

    def sibling(self):
        return self.device(self.x, self.y, self.z, 1 - self.c)

    def at(self, axis, by=0):
        if axis == "z":
            return lax.div(lax.rem(self.z + (by + 4), 4), 2)
        return lax.rem((self.x if axis == "x" else self.y) + (by + 4), 4)


def block_shape(rows, cx, cy, cz, half):
    lead = (2 if cy is None else 0, 2 if cz is None else 0, 2 if cy is None else 0, 4 if cx is None else 0)
    return tuple(v for v in lead if v) + (rows // 2 if half else rows, 128)


class Unit:
    def __init__(self, number, name, ref, lead, rlead, rows, dtype, gorder, rorder, gdirect, rdirect, place, sems, bufs):
        self.number, self.name, self.ref, self.lead, self.rlead = number, name, ref, lead, rlead
        self.rows, self.dtype, self.place = rows, dtype, place
        self.gorder, self.rorder = gorder, rorder
        self.gdirect, self.rdirect = gdirect, rdirect
        self.send, self.grecv, self.rrecv = sems
        self.bufs = bufs

    def coords(self, phase, order, v, gather):
        cur, done = order[phase], order[:phase]
        out = []
        for axis in "xyz":
            if axis == cur:
                out.append(v)
            elif (axis in done) == gather:
                out.append(None)
            else:
                out.append(self.place.at(axis))
        return out

    def index(self, cx, cy, cz, half):
        s = slice(None)
        yh, yl = (s, s) if cy is None else (lax.div(cy, 2), lax.rem(cy, 2))
        rr = s if half is None else pl.ds(half * (self.rows // 2), self.rows // 2)
        return (yh, s if cz is None else cz, yl, s if cx is None else cx, rr, s)

    def block(self, phase, order, v, half, gather):
        lead = self.lead if gather else self.rlead
        return self.ref.at[lead + self.index(*self.coords(phase, order, v, gather), half)]

    def copy(self, src, dst, phase, kind, axis, recv, by):
        k = (self.number * 3 + phase) * 4 + kind
        return pltpu.make_async_remote_copy(
            src_ref=src,
            dst_ref=dst,
            send_sem=self.send.at[k],
            recv_sem=recv.at[k],
            device_id=self.place.step(axis, by),
            device_id_type=MESH,
        )

    def way(self, kind, direct):
        if direct:
            return None, (1, -1, 2)[kind]
        return (None if kind < 2 else kind - 2), (1 if kind % 2 == 0 else -1)

    def gcopy(self, phase, kind, v):
        half, by = self.way(kind, phase in self.gdirect)
        ref = self.block(phase, self.gorder, v, half, True)
        return self.copy(ref, ref, phase, kind, self.gorder[phase], self.grecv, by)

    def gactive(self, phase, z_side):
        axis = self.gorder[phase]
        if axis == "z":
            return z_side
        return None if "z" in self.gorder[:phase] else self.place.own

    def gather1(self, phase):
        here = self.place.at(self.gorder[phase])

        def body():
            for kind in (0, 1, 2) if phase in self.gdirect else (0, 1):
                self.gcopy(phase, kind, here).start()

        when(self.gactive(phase, self.place.own), body)

    def gather2(self, phase):
        axis = self.gorder[phase]
        left, right = self.place.at(axis, -1), self.place.at(axis, 1)

        def body():
            self.gcopy(phase, 0, left).wait_recv()
            self.gcopy(phase, 2, left).start()
            self.gcopy(phase, 1, right).wait_recv()
            self.gcopy(phase, 3, right).start()

        when(self.gactive(phase, self.place.other), body)

    def gather3(self, phase):
        axis = self.gorder[phase]
        far = self.place.at(axis, 2)
        left, right = self.place.at(axis, -1), self.place.at(axis, 1)

        def near():
            self.gcopy(phase, 0, left).wait_recv()
            self.gcopy(phase, 1, right).wait_recv()

        if phase in self.gdirect:
            when(self.gactive(phase, self.place.other), near)
            when(self.gactive(phase, self.place.own), lambda: self.gcopy(phase, 2, far).wait_recv())
            return

        def body():
            self.gcopy(phase, 2, far).wait_recv()
            self.gcopy(phase, 3, far).wait_recv()

        when(self.gactive(phase, self.place.own), body)

    def gather_drain(self):
        for phase in range(3):
            here = self.place.at(self.gorder[phase])

            def sent(kinds, phase=phase, here=here):
                for kind in kinds:
                    self.gcopy(phase, kind, here).wait_send()

            if phase in self.gdirect:
                when(self.gactive(phase, self.place.own), lambda s=sent: s((0, 1, 2)))
            elif self.gorder[phase] == "z":
                when(self.place.own, lambda s=sent: s((0, 1)))
                when(self.place.other, lambda s=sent: s((2, 3)))
            else:
                when(self.gactive(phase, None), lambda s=sent: s((0, 1, 2, 3)))

    def landing(self, phase, kind):
        whole, half, lead = self.bufs[phase]
        if kind < 2 or phase in self.rdirect:
            return whole.at[lead + (kind,)]
        if self.rorder[phase] == "z":
            dims = len(whole.shape) - len(lead) - 3
            return whole.at[lead + (kind - 2,) + (slice(None),) * dims + (pl.ds(0, self.rows // 2),)]
        return half.at[lead + (kind - 2,)]

    def rcopy(self, phase, kind, v):
        half, by = self.way(kind, phase in self.rdirect)
        return self.copy(
            self.block(phase, self.rorder, v, half, False),
            self.landing(phase, kind),
            phase,
            kind,
            self.rorder[phase],
            self.rrecv,
            by,
        )

    def ractive(self, phase, z_side):
        if self.rorder[phase] == "z":
            return z_side
        return self.place.own if "z" in self.rorder[:phase] else None

    def add(self, phase, v, half, sources, out=None):
        cx, cy, cz = self.coords(phase, self.rorder, v, False)
        height = self.rows if half is None else self.rows // 2
        first = 0 if half is None else half * height
        every = slice(None)
        for yh in (0, 1) if cy is None else (lax.div(cy, 2),):
            for zi in (0, 1) if cz is None else (cz,):
                for yl in (0, 1) if cy is None else (lax.rem(cy, 2),):
                    lead = (yh,) * (cy is None) + (zi,) * (cz is None) + (yl,) * (cy is None)
                    idx = self.rlead + (yh, zi, yl, every if cx is None else cx, pl.ds(first, height))
                    if len(sources) == 1 and out is None:
                        self.ref[idx] = self.ref[idx] + sources[0][lead]
                        continue
                    total = self.ref[idx].astype(F32)
                    for src in sources:
                        total = total + src[lead].astype(F32)
                    if out is None:
                        self.ref[idx] = total.astype(self.dtype)
                    else:
                        out[...] = total

    def reduce1(self, phase):
        axis = self.rorder[phase]
        far = self.place.at(axis, 2)
        left, right = self.place.at(axis, -1), self.place.at(axis, 1)

        def body():
            self.rcopy(phase, 2, far).start()
            if phase not in self.rdirect:
                self.rcopy(phase, 3, far).start()

        when(self.ractive(phase, self.place.own), body)
        if phase in self.rdirect:

            def near():
                self.rcopy(phase, 0, right).start()
                self.rcopy(phase, 1, left).start()

            when(self.ractive(phase, self.place.other), near)

    def reduce2(self, phase):
        axis = self.rorder[phase]
        left, right = self.place.at(axis, -1), self.place.at(axis, 1)

        def body():
            self.rcopy(phase, 2, right).wait_recv()
            self.add(phase, right, 0, [self.landing(phase, 2)])
            self.rcopy(phase, 0, right).start()
            self.rcopy(phase, 3, left).wait_recv()
            self.add(phase, left, 1, [self.landing(phase, 3)])
            self.rcopy(phase, 1, left).start()

        when(self.ractive(phase, self.place.other), body)

    def reduce3(self, phase, out=None):
        here = self.place.at(self.rorder[phase])

        def body():
            kinds = (0, 1, 2) if phase in self.rdirect else (0, 1)
            for kind in kinds:
                self.rcopy(phase, kind, here).wait_recv()
            self.add(phase, here, None, [self.landing(phase, kind) for kind in kinds], out)

        when(self.ractive(phase, self.place.own), body)

    def reduce_drain(self):
        for phase in range(3):
            here = self.place.at(self.rorder[phase])

            def sent(kinds, phase=phase, here=here):
                for kind in kinds:
                    self.rcopy(phase, kind, here).wait_send()

            far = (2,) if phase in self.rdirect else (2, 3)
            if self.rorder[phase] == "z":
                when(self.place.own, lambda s=sent, far=far: s(far))
                when(self.place.other, lambda s=sent: s((0, 1)))
            else:
                when(self.ractive(phase, None), lambda s=sent, far=far: s((0, 1) + far))


class Job:
    def __init__(self, steps, backlog, latency):
        self.steps, self.backlog, self.latency, self.gate = steps, backlog, latency, None
        self.next, self.ready = 0, 0.0

    @property
    def done(self):
        return self.next == len(self.steps)


class Schedule:
    def __init__(self):
        self.now, self.busy, self.jobs = 0.0, dict(x=0.0, y=0.0, z=0.0), []

    def add(self, job):
        job.ready = self.now
        self.jobs.append(job)
        self.poll()

    def emit(self, job):
        body, axis, link, cost = job.steps[job.next]
        body()
        job.next += 1
        self.now += cost
        if axis is not None:
            self.busy[axis] = max(self.now, self.busy[axis]) + link
            job.ready = self.busy[axis] + job.latency

    def when(self, job):
        axis = job.steps[job.next][1]
        if job.gate is not None and job.next == job.gate[0] and job.gate[1].next < job.gate[2]:
            return math.inf
        if job.gate is not None and job.next == 1 and job.gate[1].next < 3:
            return math.inf
        return job.ready if axis is None else max(job.ready, self.busy[axis] - job.backlog)

    def poll(self):
        while True:
            job = next((j for j in self.jobs if not j.done and self.when(j) <= self.now), None)
            if job is None:
                return
            self.emit(job)

    def tick(self, time):
        self.now += time
        self.poll()

    def need(self, jobs):
        while not all(j.done for j in jobs):
            job = min((j for j in self.jobs if not j.done), key=self.when)
            self.now = max(self.now, self.when(job))
            self.emit(job)


def gather_steps(unit, size):
    steps = []
    for phase in range(3):
        axis, share = unit.gorder[phase], size * 5.6 / 4 ** (2 - phase)
        direct = phase in unit.gdirect

        def one(phase=phase):
            if phase:
                unit.gather3(phase - 1)
            unit.gather1(phase)

        steps.append((one, axis, share * (2 if direct else 1), 0.25))
        if not direct:
            steps.append((lambda phase=phase: unit.gather2(phase), axis, share / 2, 0.25))
    steps.append((lambda: unit.gather3(2), None, 0.0, 0.1))
    return steps


def reduce_steps(unit, size, finish):
    steps = []
    for phase in range(3):
        axis, share = unit.rorder[phase], size * 5.6 / 4 ** phase
        cost = size * 0.3 / 4 ** phase
        direct = phase in unit.rdirect

        def one(phase=phase):
            if phase:
                unit.reduce3(phase - 1)
            unit.reduce1(phase)

        steps.append((one, axis, share * (2 if direct else 0.5), 0.2 + (4 * cost if phase else 0)))
        if not direct:
            steps.append((lambda phase=phase: unit.reduce2(phase), axis, share, 0.25 + cost))
    steps.append((finish, None, 0.0, 0.3))
    return steps


ROUNDS = [("".join(reversed(o))) for o in ORDERS]


def slot(name):
    at = PLACE[name]
    return at if isinstance(at, int) else UNIT[at]


def rdirect_of(name):
    if name == "n":
        return (0, 1, 2)
    return (1, 2) if REDUCE.index(name) >= 11 else (2,)


def landing_shapes(rows, dtype, many):
    shapes = []
    for k, order in enumerate(ROUNDS if many else ROUNDS[:1]):
        for phase in range(3):
            known = order[: phase + 1]
            c = [0 if a in known else None for a in "xyz"]
            slots = 2 if many and phase == 0 else 3
            lead = (many, slots) if many else (slots,)
            shapes.append(pltpu.VMEM(lead + block_shape(rows, *c, False), dtype))
            if many and phase < 2 and order[phase] != "z":
                shapes.append(pltpu.VMEM((many, 2) + block_shape(rows, *c, True), dtype))
    return shapes


PAIR = 64


def kernel(
    tok, pos, inv, ga, gf, gq, gk, wq, wk, wv, wo, wg, wu, wd, cot,
    mixed, tgrad, fin, on,
    W, Wn, *rest,
):
    rest = list(rest)
    place = Place()
    me = place
    c = me.c
    sib = me.sibling()
    mine = pl.multiple_of(c * TOK, TOK)
    theirs = pl.multiple_of((1 - c) * TOK, TOK)
    bufs = []
    for order in ROUNDS:
        bufs.append([(rest.pop(0), rest.pop(0) if order[p] != "z" and p < 2 else None) for p in range(3)])
    nbufs = [(rest.pop(0), None, ()) for p in range(3)]
    (
        send, grecv, rrecv, lsem, psend, precv,
        X, H, FG, BG, CT, QR, KR, Q, K, VA, ATT, RL, BR, HID, ACT, H1, H2,
        COS, SIN, BIAS, PART, RECV, GROW, GQK, SM, POSM, POSR, DG, GP, GPR, FIN, FINN,
    ) = rest

    units = {}
    for i, name in enumerate(SHARD):
        k = REDUCE.index(name)
        units[name] = Unit(
            i, name, W, (i,), (slot(name),), 128, BF, ORDERS[GATHER.index(name) % 3], ROUNDS[k % 3],
            (0, 1) if GATHER.index(name) < 3 else (0,), rdirect_of(name), me, (send, grecv, rrecv), [(w, h, (k // 3,)) for w, h in bufs[k % 3]],
        )
    gains = Unit(
        NU, "n", Wn, (), (), 16, F32, ORDERS[2], ROUNDS[0], (0, 1, 2), rdirect_of("n"), me,
        (send, grecv, rrecv), nbufs,
    )
    every = list(units.values()) + [gains]

    def pair(k, src, dst):
        return pltpu.make_async_remote_copy(
            src_ref=src, dst_ref=dst, send_sem=psend.at[k], recv_sem=precv.at[k],
            device_id=sib, device_id_type=MESH,
        )

    barrier = pltpu.get_barrier_semaphore()
    for target in [me.step(a, s) for a in "xyz" for s in (1, -1, 2)] + [sib]:
        pl.semaphore_signal(barrier, inc=1, device_id=target, device_id_type=MESH)
    tok_local = pltpu.make_async_copy(tok, X.at[pl.ds(mine, TOK)], lsem.at[NU + 1])
    tok_local.start()
    cot_local = pltpu.make_async_copy(cot, CT, lsem.at[NU + 2])
    cot_local.start()
    dp = lax.axis_index("dp")
    SM[...] = jnp.zeros_like(SM)
    SM[0:1, 0:64] = ga[...].astype(F32)
    SM[1:2, 0:64] = gf[...].astype(F32)
    SM[2:3, 0:8] = gq[...].astype(F32)
    SM[3:4, 0:8] = gk[...].astype(F32)
    rows8 = lax.broadcasted_iota(jnp.int32, (8, 128), 0)
    SM[...] = jnp.where(rows8 < 2, pltpu.roll(SM[...], c * 64, 1), pltpu.roll(SM[...], dp * 8, 1))
    POSM[...] = jnp.zeros_like(POSM)
    POSM[0:2, :] = pos[...].astype(F32)
    pl.semaphore_wait(barrier, 10)

    sources = dict(q=wq, k=wk, v=wv, o=wo, g=wg, u=wu, d=wd)

    def shard(unit):
        if unit.name == "n":
            return SM
        part = int(unit.name[1:] or 0)
        return sources[unit.name[0]].at[:, pl.ds(part * 128, 128)]

    def shard_place(unit, core):
        h = unit.rows // 2
        return unit.ref.at[
            unit.lead + (me.yh, me.zi, me.yl, me.x, pl.ds(pl.multiple_of(core * h, 8), h))
        ]

    sequence = [units[n] for n in GATHER[:3]] + [gains] + [units[n] for n in GATHER[3:]]

    @pl.when(me.own)
    def _():
        for u in sequence:
            pltpu.make_async_copy(shard(u), shard_place(u, c), lsem.at[u.number]).start()

    @pl.when(me.other)
    def _():
        for u in sequence:
            pair(u.number, shard(u), shard_place(u, c)).start()

    sched = Schedule()
    jobs = {}
    for u in sequence:

        @pl.when(me.own)
        def _(u=u):
            pltpu.make_async_copy(shard(u), shard_place(u, c), lsem.at[u.number]).wait()
            pair(u.number, shard_place(u, 1 - c), shard_place(u, 1 - c)).wait_recv()

        jobs[u.name] = Job(gather_steps(u, 0.02 if u is gains else 1.0), GATHER_BACKLOG, LATENCY)
        at = GATHER.index(u.name) - 3 * AHEAD if u is not gains else -1
        if at >= 0:
            before = jobs[GATHER[at]]
            jobs[u.name].gate = (len(jobs[u.name].steps) - 3, before, len(before.steps) - 1)
        sched.add(jobs[u.name])

    pos_pair = pair(NU + 1, POSM, POSR)
    pos_pair.start()
    tok_pair = pair(NU + 2, tok, X.at[pl.ds(mine, TOK)])
    tok_pair.start()
    sched.tick(0.8)

    @pl.when(me.other)
    def _():
        for u in sequence:
            pair(u.number, shard(u), shard_place(u, c)).wait_send()

    pos_pair.wait()

    lane = lax.broadcasted_iota(jnp.int32, (128, 128), 1)
    slots = lax.broadcasted_iota(jnp.int32, (128, 256), 1)
    rows2 = lax.broadcasted_iota(jnp.int32, (128, 256), 0)
    inv_row = jnp.broadcast_to(inv[...][:1], (128, 128))

    def tables(b, h):
        place_row = jnp.where(c == b, POSM[h : h + 1, :], POSR[h : h + 1, :])
        places = jnp.broadcast_to(place_row, (128, 128)).T
        angles = places * inv_row
        rs = pl.ds(b * 256 + h * 128, 128)
        COS[rs, :] = jnp.cos(angles)
        sine = jnp.sin(angles)
        SIN[rs, :] = jnp.where(lane < 64, -sine, sine)
        t = rows2 + h * 128
        first = t - jnp.concatenate([places, places], axis=1).astype(jnp.int32)
        allowed = (slots <= t) & (slots >= first)
        bias = jnp.where(allowed, 0.0, -1e30)
        BIAS[b, pl.ds(h * 128, 128), :] = bias

    for b in range(2):
        for h in range(2):
            tables(b, h)
            sched.tick(0.5)
    ones = jnp.ones((256, 128), BF)
    with_ones = lambda f, b: jnp.concatenate([VA[f, b], ones], axis=1)
    tok_local.wait()
    tok_pair.wait()
    cot_local.wait()

    def full(u, yh):
        return [W[UNIT[u] if isinstance(u, str) else u, yh, zi].reshape(1024, 128) for zi in range(2)]

    def wide(u):
        return jnp.concatenate(full(u, 0) + full(u, 1), axis=1)

    def tile(names, yh, j):
        at = lambda u, zi: W[UNIT[u], yh, zi, j // 2, pl.ds(j % 2 * 2, 2)].reshape(256, 128)
        return jnp.concatenate([at(u, zi) for u in names for zi in range(2)], axis=1)

    def turn(v):
        return pltpu.roll(v, 64, 1)

    def normed(v, gain, b):
        rs = pl.ds(b * 256, 256)
        v = v * lax.rsqrt(jnp.mean(v * v, axis=-1, keepdims=True) + EPS) * gain
        return (v * COS[rs, :] + turn(v) * SIN[rs, :]).astype(BF)

    sched.need([jobs[n] for n in ("q0", "q1", "k", "n")])
    for j in range(8):
        for r in range(2):
            GROW[r : r + 1, j * 128 : (j + 1) * 128] = (
                Wn[0, 0, j // 4, j % 4, r : r + 1, :] + Wn[0, 0, j // 4, j % 4, 8 + r : 9 + r, :]
            )
    gq = jnp.zeros((8, 128), F32)
    for j in range(8):
        gq = gq + Wn[0, 0, j // 4, j % 4, 0:8, :] + Wn[0, 0, j // 4, j % 4, 8:16, :]
    GQK[...] = gq
    qgain = GQK[2:3, :]
    kgain = GQK[3:4, :]
    sched.tick(0.3)

    def heads(raw):
        for b in range(2):
            for f in range(4):
                yield b, f, raw[b * 256 : b * 256 + 256, f * 128 : f * 128 + 128]

    def queries(r, carry):
        raw = nn(X[...], wide(r))
        for b, f, v in heads(raw):
            QR[f // 2, r, pl.ds(b * 256, 256), pl.ds(f % 2 * 128, 128)] = v.astype(BF)
            Q[f, b, pl.ds(pl.multiple_of(r * 256, 256), 256), :] = normed(v, qgain, b)
        return carry

    lax.fori_loop(0, 2, queries, 0)
    sched.tick(2.4)
    raw = nn(X[...], wide("k"))
    for b, f, v in heads(raw):
        KR[f // 2, pl.ds(b * 256, 256), pl.ds(f % 2 * 128, 128)] = v.astype(BF)
        K[f, b] = normed(v, kgain, b)
    sched.tick(1.2)

    sched.need([jobs["v"]])
    raw = nn(X[...], wide("v")).astype(BF)
    for f in range(4):
        for b in range(2):
            VA[f, b] = raw[b * 256 : b * 256 + 256, f * 128 : f * 128 + 128]
    sched.tick(0.8)

    scale = HD ** -0.5
    power = scale * math.log2(math.e)

    def attend(f, b):
        yh, zi = f // 2, f % 2
        rs = pl.ds(b * 256, 256)
        for r in range(2):
            s = nt(Q[f, b, pl.ds(r * 256, 256), :], K[f, b])
            e = jnp.exp2(s * power + BIAS[b]).astype(BF)
            ol = nn(e, with_ones(f, b))
            rl = 1.0 / ol[:, 128:256]
            at = pl.ds(r * 256 + zi * 128, 128)
            ATT[yh, rs, at] = (ol[:, 0:128] * rl).astype(BF)
            RL[yh, rs, at] = rl.astype(BF)

    for f in range(4):
        for b in range(2):
            attend(f, b)
            sched.tick(0.35)

    for b in range(2):
        BIAS[b] = BIAS[b].T

    def pair_piece(base, slot, j):
        cols = pl.ds(j * 256, 256)
        return pair(base + j, PART.at[0, :, cols], RECV.at[slot, :, cols])

    def pair_sum(base, slot, products, time):
        def one(rows, j):
            out = None
            for left, names, yh in products:
                p = nt(left(rows), tile(names, yh, j))
                out = p if out is None else out + p
            return out

        def side(i, carry):
            rows = pl.ds(pl.multiple_of(lax.rem(1 - c + i, 2) * TOK, TOK), TOK)
            for j in range(4):
                PART[i, :, pl.ds(j * 256, 256)] = one(rows, j).astype(BF)
                if j % 2:

                    @pl.when(i == 0)
                    def _(j=j):
                        pair_piece(base, slot, j - 1).start()
                        pair_piece(base, slot, j).start()

            return carry

        lax.fori_loop(0, 2, side, 0)
        sched.tick(2 * time)

    def pair_done(base, slot):
        for j in range(4):
            pair_piece(base, slot, j).wait()

    CH = 64

    def rows_then_send(base, dst, body):
        for j in range(TOK // CH):
            rs = pl.ds(pl.multiple_of(mine + j * CH, CH), CH)
            body(pl.ds(j * CH, CH), rs)
            pair(base + j, dst.at[rs], dst.at[rs]).start()
        sched.tick(0.5)

    def rows_done(base, dst):
        for j in range(TOK // CH):
            rs = pl.ds(pl.multiple_of(mine + j * CH, CH), CH)
            pair(base + j, dst.at[rs], dst.at[rs]).wait_send()
            rs = pl.ds(pl.multiple_of(theirs + j * CH, CH), CH)
            pair(base + j, dst.at[rs], dst.at[rs]).wait_recv()

    sched.need([jobs["o0"], jobs["o1"]])

    pair_sum(
        20, 0, [(lambda rows, yh=yh: ATT[yh, rows, :], ("o0", "o1"), yh) for yh in range(2)], 0.8
    )
    pair_done(20, 0)

    def hidden_rows(rs, abs_rs):
        v = PART[1, rs, :].astype(F32) + RECV[0, rs, :].astype(F32)
        BR[rs, :] = v
        n = v * lax.rsqrt(jnp.mean(v * v, axis=-1, keepdims=True) + EPS) * GROW[0:1, :]
        hid = X[abs_rs, :].astype(F32) + n
        HID[rs, :] = hid
        H[abs_rs, :] = hid.astype(BF)

    rows_then_send(24, H, hidden_rows)

    def ffn_tile(s, rows):
        h = H[rows, :]
        g = nn(h, wide("g%d" % s))
        u = nn(h, wide("u%d" % s))
        sg = 0.5 * jnp.tanh(0.5 * g) + 0.5
        silu = g * sg
        act = (silu * u).astype(BF)
        h1 = ((sg + silu * (1.0 - sg)) * u).astype(BF)
        h2 = silu.astype(BF)
        for yh in range(2):
            cols, part = pl.ds(s * 256, 256), slice(yh * 256, yh * 256 + 256)
            ACT[yh, rows, cols] = act[:, part]
            H1[yh, rows, cols] = h1[:, part]
            H2[yh, rows, cols] = h2[:, part]

    sched.need([jobs["g0"], jobs["u0"]])

    def first_tiles(i, carry):
        @pl.when(i == 1)
        def _():
            rows_done(24, H)

        ffn_tile(0, pl.ds(pl.multiple_of(lax.rem(c + i, 2) * TOK, TOK), TOK))
        return carry

    lax.fori_loop(0, 2, first_tiles, 0)
    sched.tick(1.5)
    for s in (1, 2):
        sched.need([jobs["g%d" % s], jobs["u%d" % s]])

        def tiles(m, carry, s=s):
            ffn_tile(s, pl.ds(pl.multiple_of(m * 256, 256), 256))
            return carry

        lax.fori_loop(0, 2, tiles, 0)
        sched.tick(1.5)
    for u in every:
        if u.name[0] != "d":
            u.gather_drain()
    sched.need([jobs["d%d" % s] for s in range(3)])
    pair_sum(
        28, 1, [(lambda rows, yh=yh: ACT[yh, rows, :], ("d0", "d1", "d2"), yh) for yh in range(2)], 1.1
    )
    DG[...] = jnp.zeros_like(DG)
    GP[...] = jnp.zeros_like(GP)
    for n in ("d0", "d1", "d2"):
        units[n].gather_drain()
    pair_done(28, 1)

    def rms_back(v, r, gain, dn, at):
        gd = gain * dn
        vr = v * r
        grad = r * (gd - vr * jnp.mean(gd * vr, axis=-1, keepdims=True))
        dg = dn * vr
        DG[at, :, :] += jnp.sum(dg.reshape(CH // 8, 8, 1024), axis=0)
        return grad

    def ffn_rows(rs, abs_rs):
        v = PART[1, rs, :].astype(F32) + RECV[1, rs, :].astype(F32)
        gain = GROW[1:2, :]
        r = lax.rsqrt(jnp.mean(v * v, axis=-1, keepdims=True) + EPS)
        PART[0, rs, :] = (HID[rs, :] + v * r * gain).astype(BF)
        FG[abs_rs, :] = rms_back(v, r, gain, CT[rs, :].astype(F32), 1).astype(BF)

    rows_then_send(32, FG, ffn_rows)
    mixed_out = pltpu.make_async_copy(PART.at[0], mixed, lsem.at[0])
    mixed_out.start()

    def weight_grad(u, left, right):
        def half(j, carry):
            cols = pl.ds(pl.multiple_of(j * 512, 512), 512)
            out = tn(left[:, cols], jnp.concatenate([right(0), right(1)], axis=1)).astype(BF)
            for yh in range(2):
                for zi in range(2):
                    at = (yh * 2 + zi) * 128
                    W[slot(u), yh, zi, j] = out[:, at : at + 128].reshape(4, 128, 128)
            return carry

        lax.fori_loop(0, 2, half, 0)

    fin_jobs = []

    def start_reduce(u):
        unit = gains if u == "n" else units[u]
        out = FINN if u == "n" else FIN.at[unit.number]

        def finish():
            unit.reduce3(2, out)

            @pl.when(me.own)
            def _():
                fin_pair(unit, 1 - c).start()

            unit.reduce_drain()

        job = Job(reduce_steps(unit, 0.02 if u == "n" else 1.0, finish), REDUCE_BACKLOG, REDUCE_LATENCY)
        fin_jobs.append(job)
        sched.add(job)

    def fin_pair(unit, core):
        if unit.name == "n":
            ref = FINN
        else:
            ref = FIN.at[unit.number, pl.ds(pl.multiple_of(core * 64, 64), 64)]
        return pair(48 + unit.number, ref, ref)

    def act_back(s, rs, time):
        cols = pl.ds(s * 256, 256)
        da = nn(FG[rs, :], wide("d%d" % s))
        for yh in range(2):
            part = da[:, yh * 256 : yh * 256 + 256]
            H1[yh, rs, cols] = (part * H1[yh, rs, cols].astype(F32)).astype(BF)
            H2[yh, rs, cols] = (part * H2[yh, rs, cols].astype(F32)).astype(BF)
        sched.tick(time)

    for s in range(3):
        act_back(s, pl.ds(mine, TOK), 0.0)
    rows_done(32, FG)

    def down(u):
        weight_grad(u, FG, lambda yh: ACT[yh, :, pl.ds(int(u[1]) * 256, 256)])
        sched.tick(0.85)
        start_reduce(u)

    def gate_up(u):
        cols = pl.ds(int(u[1]) * 256, 256)
        part = H1 if u[0] == "g" else H2
        weight_grad(u, H, lambda yh: part[yh, :, cols])
        sched.tick(0.85)
        start_reduce(u)

    down("d0")
    down("d1")
    act_back(0, pl.ds(theirs, TOK), 0.45)
    down("d2")
    act_back(1, pl.ds(theirs, TOK), 0.45)
    gate_up("g0")
    act_back(2, pl.ds(theirs, TOK), 0.45)
    gate_up("u0")
    mixed_out.wait()
    pair_sum(
        36, 0,
        [(lambda rows, yh=yh: H1[yh, rows, :], ("g0", "g1", "g2"), yh) for yh in range(2)]
        + [(lambda rows, yh=yh: H2[yh, rows, :], ("u0", "u1", "u2"), yh) for yh in range(2)],
        2.2,
    )
    gate_up("g1")
    gate_up("u1")
    pair_done(36, 0)

    def branch_rows(rs, abs_rs):
        dn = CT[rs, :].astype(F32) + PART[1, rs, :].astype(F32) + RECV[0, rs, :].astype(F32)
        HID[rs, :] = dn
        v = BR[rs, :]
        r = lax.rsqrt(jnp.mean(v * v, axis=-1, keepdims=True) + EPS)
        BG[abs_rs, :] = rms_back(v, r, GROW[0:1, :], dn, 0).astype(BF)

    rows_then_send(40, BG, branch_rows)
    gate_up("g2")
    gate_up("u2")
    rows_done(40, BG)

    DO = FG
    for r in range(2):
        out = nn(BG[...], wide("o%d" % r)).astype(BF)
        for yh in range(2):
            DO[:, pl.ds(yh * 512 + r * 256, 256)] = out[:, yh * 256 : yh * 256 + 256]
        sched.tick(0.8)
    for r in range(2):
        weight_grad("o%d" % r, BG, lambda yh: ATT[yh, :, pl.ds(r * 256, 256)])
        sched.tick(0.85)
        start_reduce("o%d" % r)

    def head_back(raw, gain, d, rs, row_at):
        d = d * COS[rs, :] - turn(d) * SIN[rs, :]
        r = lax.rsqrt(jnp.mean(raw * raw, axis=-1, keepdims=True) + EPS)
        gd = gain * d
        vr = raw * r
        GP[pl.ds(row_at, 8), :] += jnp.sum((d * vr).reshape(32, 8, 128), axis=0)
        return (r * (gd - vr * jnp.mean(gd * vr, axis=-1, keepdims=True))).astype(BF)

    QG, KVG = ACT, H1

    def attend_back(zi, n):
        yh, b = lax.div(n, 2), lax.rem(n, 2)
        f = yh * 2 + zi
        rs = pl.ds(pl.multiple_of(b * 256, 256), 256)
        dk, dv = None, None
        for r in range(2):
            at = pl.ds(r * 256 + zi * 128, 128)
            q = Q[f, b, pl.ds(r * 256, 256), :]
            do = DO[rs, pl.ds(pl.multiple_of(yh * 512 + (r * 256 + zi * 128), 128), 128)]
            do = do.astype(F32) * RL[yh, rs, at].astype(F32)
            dol = do.astype(BF)
            doa = jnp.concatenate([dol, (-(do * ATT[yh, rs, at].astype(F32))).astype(BF)], axis=1)
            e = jnp.exp2(nt(K[f, b], q) * power + BIAS[b])
            ds = (e * nt(with_ones(f, b), doa)).astype(BF)
            dv_r = nn(e.astype(BF), dol)
            dk_r = nn(ds, q)
            dv = dv_r if dv is None else dv + dv_r
            dk = dk_r if dk is None else dk + dk_r
            dq = tn(ds, K[f, b]) * scale
            raw = QR[yh, r, rs, pl.ds(zi * 128, 128)].astype(F32)
            QG[yh, rs, at] = head_back(raw, qgain, dq, rs, 0)
        raw = KR[yh, rs, pl.ds(zi * 128, 128)].astype(F32)
        KVG[yh, rs, pl.ds(zi * 128, 128)] = head_back(raw, kgain, dk * scale, rs, 8)
        KVG[yh, rs, pl.ds(256 + zi * 128, 128)] = dv.astype(BF)

    for zi in range(2):

        def back(n, carry, zi=zi):
            attend_back(zi, n)
            return carry

        lax.fori_loop(0, 4, back, 0)
        sched.tick(4.0)

    def gain_rows(at, row_at):
        summed = jnp.sum(DG[at], axis=0, keepdims=True)
        for j in range(8):
            GP[row_at + j : row_at + j + 1, :] = summed[:, j * 128 : (j + 1) * 128]

    qsum = jnp.sum(GP[0:8, :], axis=0, keepdims=True)
    ksum = jnp.sum(GP[8:16, :], axis=0, keepdims=True)
    gain_rows(0, 16)
    gain_rows(1, 24)
    GP[0:1, :] = qsum
    GP[8:9, :] = ksum
    gain_pair = pair(NU + 3, GP, GPR)
    gain_pair.start()

    def proj_grad(u, src, at):
        weight_grad(u, X, lambda yh: src[yh, :, pl.ds(at, 256)])
        sched.tick(0.85)
        start_reduce(u)

    proj_grad("q0", QG, 0)
    proj_grad("q1", QG, 256)
    proj_grad("k", KVG, 0)
    proj_grad("v", KVG, 256)
    gain_pair.wait()
    GPR[...] += GP[...]
    Wn[...] = jnp.zeros_like(Wn)
    for j in range(8):
        for f0 in range(2):
            for f1 in range(2):
                Wn[f0, f1, j // 4, j % 4, 0:1, :] = GPR[16 + j : 17 + j, :]
                Wn[f0, f1, j // 4, j % 4, 1:2, :] = GPR[24 + j : 25 + j, :]
                Wn[f0, f1, j // 4, j % 4, 8:9, :] = GPR[0:1, :]
                Wn[f0, f1, j // 4, j % 4, 9:10, :] = GPR[8:9, :]
    start_reduce("n")
    pair_sum(
        44, 1,
        [(lambda rows, yh=yh: QG[yh, rows, pl.ds(0, 512)], ("q0", "q1"), yh) for yh in range(2)]
        + [(lambda rows, yh=yh: KVG[yh, rows, pl.ds(0, 512)], ("k", "v"), yh) for yh in range(2)],
        1.4,
    )
    pair_done(44, 1)

    for j in range(TOK // CH):
        rs = pl.ds(j * CH, CH)
        HID[rs, :] = HID[rs, :] + PART[1, rs, :].astype(F32) + RECV[1, rs, :].astype(F32)
    tgrad_out = pltpu.make_async_copy(HID, tgrad, lsem.at[1])
    tgrad_out.start()
    sched.tick(0.6)

    sched.need(fin_jobs)
    for u in every:

        @pl.when(me.own)
        def _(u=u):
            fin_pair(u, 1 - c).wait_send()

        @pl.when(me.other)
        def _(u=u):
            fin_pair(u, c).wait_recv()

    mrows = pl.ds(pl.multiple_of(c * 64, 64), 64)
    fin_out = pltpu.make_async_copy(FIN.at[:, mrows], fin, lsem.at[2])
    fin_out.start()
    on_out = pltpu.make_async_copy(FINN, on, lsem.at[3])
    on_out.start()
    tgrad_out.wait()
    fin_out.wait()
    on_out.wait()


def finish_kernel(mixed_in, tgrad_in, fin, gn, mixed, tgrad, oq, ok, ov, oo, og, ou, od, oqg, okg, oag, ofg, sem):
    dp = lax.axis_index("dp")
    core = lax.rem(dp, 2)
    copies = [(mixed_in, mixed), (tgrad_in, tgrad)]
    targets = dict(q=oq, k=ok, v=ov, o=oo, g=og, u=ou, d=od)
    for i, name in enumerate(SHARD):
        part = int(name[1:] or 0)
        copies.append((fin.at[i], targets[name[0]].at[:, pl.ds(part * 128, 128)]))
    copies = [pltpu.make_async_copy(a, b, sem.at[i]) for i, (a, b) in enumerate(copies)]
    for copy in copies:
        copy.start()
    odd = core == 1
    for ref, row in ((oag, 0), (ofg, 1)):
        v = gn[...]
        v = jnp.where(odd, pltpu.roll(v, 64, 1), v)
        ref[...] = v[row : row + 1, 0:64]
    v = gn[...]
    back = lax.rem(128 - dp * 8, 128)
    v = pltpu.roll(v, back, 1)
    oqg[...] = v[8:9, 0:8]
    okg[...] = v[9:10, 0:8]
    for copy in copies:
        copy.wait()


def on_device(
    tokens, positions, w_query, w_key, w_value, w_out, w_gate, w_up, w_down,
    query_gain, key_gain, attn_gain, ffn_gain, cotangent,
):
    steps_up = np.arange(0, HD, 2).astype(np.float32) / np.float32(HD)
    inverse = (np.float32(ROPE_BASE) ** (-steps_up)).astype(np.float32)
    inv = jnp.asarray(np.tile(np.concatenate([inverse, inverse])[None], (8, 1)))
    vm = pl.BlockSpec(memory_space=pltpu.VMEM)
    hbm = pl.BlockSpec(memory_space=pl.ANY)
    far = pl.BlockSpec(memory_space=pltpu.HBM)
    n = (NU + 1) * 12
    V = pltpu.VMEM
    sems = [pltpu.SemaphoreType.DMA((n,))] * 3 + [
        pltpu.SemaphoreType.DMA((NU + 3,)),
        pltpu.SemaphoreType.DMA((PAIR,)),
        pltpu.SemaphoreType.DMA((PAIR,)),
    ]
    work = [
        V((512, D), BF), V((512, D), BF), V((512, D), BF), V((512, D), BF),
        V((TOK, D), BF),
        V((2, 2, 512, 256), BF), V((2, 512, 256), BF),
        V((4, 2, 512, 128), BF), V((4, 2, 256, 128), BF), V((4, 2, 256, 128), BF),
        V((2, 512, 512), BF), V((2, 512, 512), BF),
        V((TOK, D), F32), V((TOK, D), F32),
        V((2, 512, 768), BF), V((2, 512, 768), BF), V((2, 512, 768), BF),
        V((512, 128), F32), V((512, 128), F32), V((2, 256, 256), F32),
        V((2, TOK, D), BF), V((2, TOK, D), BF),
        V((8, D), F32), V((8, 128), F32), V((8, 128), F32), V((8, 128), F32), V((8, 128), F32), V((2, 8, D), F32),
        V((32, 128), F32), V((32, 128), F32),
        V((NU, 128, 128), F32), V((16, 128), F32),
    ]
    f = lambda *s: jax.ShapeDtypeStruct(s, F32)
    main_out = pl.pallas_call(
        kernel,
        out_shape=(jax.ShapeDtypeStruct((TOK, D), BF), f(TOK, D), f(NU, 64, 128), f(16, 128)),
        in_specs=[hbm] + [vm] * 6 + [hbm] * 8,
        out_specs=[hbm] * 4,
        scratch_shapes=[V((NU + SPARE, 2, 2, 2, 4, 128, 128), BF), V((2, 2, 2, 4, 16, 128), F32)]
        + landing_shapes(128, BF, 5) + landing_shapes(16, F32, 0) + sems + work,
        compiler_params=pltpu.CompilerParams(
            collective_id=1, has_side_effects=True, vmem_limit_bytes=int(63.5 * 2**20)
        ),
        cost_estimate=pl.CostEstimate(flops=26 * 10**9, bytes_accessed=4 * 10**6, transcendentals=0),
    )(
        tokens, positions.reshape(2, 128), inv,
        attn_gain.reshape(1, 64), ffn_gain.reshape(1, 64), query_gain.reshape(1, 8), key_gain.reshape(1, 8),
        w_query, w_key, w_value, w_out.T, w_gate, w_up, w_down.T, cotangent,
    )
    outs = pl.pallas_call(
        finish_kernel,
        out_shape=(
            jax.ShapeDtypeStruct((TOK, D), BF), f(TOK, D),
            f(64, 256), f(64, 128), f(64, 128), f(64, 256), f(64, 384), f(64, 384), f(64, 384),
            f(1, 8), f(1, 8), f(1, 64), f(1, 64),
        ),
        in_specs=[vm] * 4,
        out_specs=[far] * 9 + [vm] * 4,
        scratch_shapes=[pltpu.SemaphoreType.DMA((NU + 2,))],
        compiler_params=pltpu.CompilerParams(vmem_limit_bytes=int(63.5 * 2**20)),
    )(*main_out)
    mixed, tgrad, gq, gk, gv, go, gg, gu, gd, nq, nk, na, nf = outs
    return (
        mixed, tgrad, gq, gk, gv, go.T, gg, gu, gd.T,
        nq.reshape(8), nk.reshape(8), na.reshape(64), nf.reshape(64),
    )


def solution(mesh):
    both, w, wt = P(("dp", "fsdp"), None), P("dp", "fsdp"), P("fsdp", "dp")
    return jax.shard_map(
        on_device,
        mesh=mesh,
        in_specs=(both, P(("dp", "fsdp")), w, w, w, wt, w, w, wt, P("dp"), P("dp"), P("dp"), P("dp"), both),
        out_specs=(both, both, w, w, w, wt, w, w, wt, P("dp"), P("dp"), P("dp"), P("dp")),
        check_vma=False,
    )
```

profile of v0, /device:TPU:1, one launch (start us, length us, event | category | flops | bytes accessed | tf_op | source)
XLA Modules:
  0.0 165.8 jit_solution(877218233714537699)
XLA Ops:
  0.7 161.5 %shard_map.246 = (bf16[256,1024]{1,0:T(8,128)(2,1)}, f32[256,1024]{1,0:T(8,128)}, f32[15,64,128]{2,1,0:T(8,128)}, f32[16,128]{1,0:T(8,128)}) custom-call(bf16[256,1024]{1,0:T(8,128)(2,1)} %tok.1, s32[2,128]{1,0:T(2,128)} %bitcast.17, f32[8,128]{1,0:T(8,128)} %constant.2.clone.inv, bf16[1,64]{1,0:T(2,128)(2,1)} %bitcast.18, bf16[1,64]{1,0:T(2,128)(2,1)} %bitcast.19, ...), custom_call_target="tpu_custom_call" | custom-call | flops 25999998976 | bytes 4000000 | tf_op jit(solution)/shard_map/pallas_call | solution.py:1068
  162.2 3.5 %shard_map.247 = (bf16[256,1024]{1,0:T(8,128)(2,1)}, f32[256,1024]{1,0:T(8,128)}, f32[64,256]{1,0:T(8,128)}, f32[64,128]{1,0:T(8,128)}, f32[64,128]{1,0:T(8,128)...) custom-call(bf16[256,1024]{1,0:T(8,128)(2,1)} %get-tuple-element.30., ...), custom_call_target="tpu_custom_call" | custom-call | tf_op jit(solution)/shard_map/pallas_call | solution.py:1084
where the time goes:
time: 166 us
  Pallas kernels  165 us (99%)
    pallas_call x1, Pallas kernels, on_device(): pl.pallas_call(kernel, out_shape=(jax.ShapeDtypeStruct((TOK, D), BF), f(T...  162 us
    pallas_call x1, Pallas kernels, on_device(): pl.pallas_call(finish_kernel, out_shape=(jax.ShapeDtypeStruct((TOK, D), B...  3.48 us

commit v1 on v0

--- a/solution.py
+++ b/solution.py
@@ -20,7 +20,7 @@
 UNIT = {name: i for i, name in enumerate(SHARD)}
 NU = len(SHARD)
 LATENCY, REDUCE_LATENCY = 2.6, 10.0
-GATHER_BACKLOG, REDUCE_BACKLOG, AHEAD = 1000.0, 6.0, 2
+GATHER_BACKLOG, REDUCE_BACKLOG, AHEAD = 1000.0, 6.0, 3
 SPARE = 4
 PLACE = dict(
     d0=15, d1=16, d2="d0", g0="d1", u0="d2", g1="g0", u1="u0", g2="g1", u2="u1", o0="g2", o1="u2", q0="o0", q1="o1",

time: 166 us -> 163 us (0.982)
  Pallas kernels: 165 us -> 162 us
    pallas_call x1, Pallas kernels: 162 us -> 158 us  [on_device(): pl.pallas_call(kernel, out_shape=(jax.ShapeDtypeStruct((TOK, D), BF), f(T...]
where the time goes in v1:
time: 163 us
  Pallas kernels  162 us (99%)
    pallas_call x1, Pallas kernels, on_device(): pl.pallas_call(kernel, out_shape=(jax.ShapeDtypeStruct((TOK, D), BF), f(T...  158 us
    pallas_call x1, Pallas kernels, on_device(): pl.pallas_call(finish_kernel, out_shape=(jax.ShapeDtypeStruct((TOK, D), B...  3.48 us

profile of v1, /device:TPU:1, one launch (start us, length us, event | category | flops | bytes accessed | tf_op | source)
XLA Modules:
  0.0 162.6 jit_solution(13458051910158455799)
XLA Ops:
  0.7 158.2 %shard_map.246 = (bf16[256,1024]{1,0:T(8,128)(2,1)}, f32[256,1024]{1,0:T(8,128)}, f32[15,64,128]{2,1,0:T(8,128)}, f32[16,128]{1,0:T(8,128)}) custom-call(bf16[256,1024]{1,0:T(8,128)(2,1)} %tok.1, s32[2,128]{1,0:T(2,128)} %bitcast.17, f32[8,128]{1,0:T(8,128)} %constant.2.clone.inv, bf16[1,64]{1,0:T(2,128)(2,1)} %bitcast.18, bf16[1,64]{1,0:T(2,128)(2,1)} %bitcast.19, ...), custom_call_target="tpu_custom_call" | custom-call | flops 25999998976 | bytes 4000000 | tf_op jit(solution)/shard_map/pallas_call | solution.py:1068
  158.9 3.5 %shard_map.247 = (bf16[256,1024]{1,0:T(8,128)(2,1)}, f32[256,1024]{1,0:T(8,128)}, f32[64,256]{1,0:T(8,128)}, f32[64,128]{1,0:T(8,128)}, f32[64,128]{1,0:T(8,128)...) custom-call(bf16[256,1024]{1,0:T(8,128)(2,1)} %get-tuple-element.30., ...), custom_call_target="tpu_custom_call" | custom-call | tf_op jit(solution)/shard_map/pallas_call | solution.py:1084
